TPU v7x, 32 devices: a whole 2x2x4 slice. The times are simulated.
32 devices in a mesh: dp: 16 (over z, y, x), mp: 2 (over core).
Axes of the slice: x: 2, y: 2, z: 4, core: 2. Of those that a mesh axis runs over, the one named last changes fastest.
Arguments:
- pool_images: bfloat16 [128, 196, 768], P('dp'), may hold values from -6 to 6
- pick_rows: int32 [128], P('dp'), may hold values from 0 to 7
- pick_weight: int32 [128], P('dp'), may hold values from 1 to 8
- pick_label: int32 [128], P('dp'), may hold values from 0 to 999
- in_proj: float32 [2, 384, 1152], P('mp', None, 'dp'), may hold values from -0.3125 to 0.3125
- out_proj: float32 [2, 384, 384], P('mp', None, 'dp'), may hold values from -2 to 2
- up_proj: float32 [2, 384, 1536], P('mp', None, 'dp'), may hold values from -0.3125 to 0.3125
- down_proj: float32 [2, 384, 1536], P('mp', None, 'dp'), may hold values from -0.15625 to 0.15625
- in_moment: float32 [2, 384, 1152], P('mp', None, 'dp'), may hold values from -3.0517578e-05 to 3.0517578e-05
- out_moment: float32 [2, 384, 384], P('mp', None, 'dp'), may hold values from -3.0517578e-05 to 3.0517578e-05
- up_moment: float32 [2, 384, 1536], P('mp', None, 'dp'), may hold values from -3.0517578e-05 to 3.0517578e-05
- down_moment: float32 [2, 384, 1536], P('mp', None, 'dp'), may hold values from -3.0517578e-05 to 3.0517578e-05
- patch_embed: float32 [768, 384], P('dp'), may hold values from -0.21875 to 0.21875
- class_head: float32 [384, 1000], P('dp'), may hold values from -0.625 to 0.625
- pos_table: float32 [384, 197], P('dp'), may hold values from -3 to 3
- norm_params: float32 [384, 10], P('dp'), may hold values from -1 to 4, as said below
- patch_first: float32 [768, 384], P('dp'), may hold values from -3.33786e-06 to 3.33786e-06
- head_first: float32 [384, 1000], P('dp'), may hold values from -3.33786e-06 to 3.33786e-06
- pos_first: float32 [384, 197], P('dp'), may hold values from -3.33786e-06 to 3.33786e-06
- norm_first: float32 [384, 10], P('dp'), may hold values from -1.335144e-05 to 1.335144e-05
- patch_second: float32 [768, 384], P('dp'), may hold values from 1.23332e-12 to 4.93328e-12
- head_second: float32 [384, 1000], P('dp'), may hold values from 1.23332e-12 to 4.93328e-12
- pos_second: float32 [384, 197], P('dp'), may hold values from 1.23332e-12 to 4.93328e-12
- norm_second: float32 [384, 10], P('dp'), may hold values from 1.9779659e-11 to 7.9118635e-11
Outputs:
- loss_total: float32 [], replicated
- weight_total: float32 [], replicated
- grad_norm: float32 [], replicated
- pool_score: float32 [128], P(('dp', 'mp'))
- new_in_proj: float32 [2, 384, 1152], P('mp', None, 'dp')
- new_out_proj: float32 [2, 384, 384], P('mp', None, 'dp')
- new_up_proj: float32 [2, 384, 1536], P('mp', None, 'dp')
- new_down_proj: float32 [2, 384, 1536], P('mp', None, 'dp')
- new_in_moment: float32 [2, 384, 1152], P('mp', None, 'dp')
- new_out_moment: float32 [2, 384, 384], P('mp', None, 'dp')
- new_up_moment: float32 [2, 384, 1536], P('mp', None, 'dp')
- new_down_moment: float32 [2, 384, 1536], P('mp', None, 'dp')
- new_patch_embed: float32 [768, 384], P('dp')
- new_class_head: float32 [384, 1000], P('dp')
- new_pos_table: float32 [384, 197], P('dp')
- new_norm_params: float32 [384, 10], P('dp')
- new_patch_first: float32 [768, 384], P('dp')
- new_head_first: float32 [384, 1000], P('dp')
- new_pos_first: float32 [384, 197], P('dp')
- new_norm_first: float32 [384, 10], P('dp')
- new_patch_second: float32 [768, 384], P('dp')
- new_head_second: float32 [384, 1000], P('dp')
- new_pos_second: float32 [384, 197], P('dp')
- new_norm_second: float32 [384, 10], P('dp')
Inputs may be any that keep to these rules, and one draw needn't show every extreme that they name: `pick_rows`: an index into the 8 pool images of the same block of dp. `norm_params`: even columns are gains, positive; odd columns are biases.
All inputs are finite; a program needn't handle non-finite values.
Results may differ from a plain program's by a relative error of at most 0.0095.
The roundings to bfloat16 on the way count: a program that leaves them out, or rounds other values in their place, can miss the bound.
Values may be sent and summed in bfloat16 or wider, within the bound.
A program may use at most 256 MiB of HBM per device.

v0:
```python
from functools import partial
import math

import jax
import jax.numpy as jnp
from jax import lax
from jax.sharding import PartitionSpec as P

HEAD_DIM = 64
MB = 2
STEP = 5


PRECISE = lax.Precision.HIGHEST
EPSILON = 1e-06
NS_A = 3.4445
NS_B = -4.775
NS_C = 2.0315
MOMENTUM = 0.95
MUON_RATES = (0.1, 0.4, 0.1, 0.1)
DECAY = 0.01
BETA_ONE = 0.9
BETA_TWO = 0.95
ADAM_EPS = 1e-08
ADAM_RATES = (0.01, 0.02, 0.1, 0.2)
THRESHOLD = 0.01
BF = jnp.bfloat16
FL = jnp.float32


def layer_norm(values, norm_gain, norm_bias):
    average = jnp.mean(values, -1, keepdims=True)
    centered = values - average
    variance = jnp.mean(centered * centered, -1, keepdims=True)
    return centered * lax.rsqrt(variance + EPSILON) * norm_gain + norm_bias


def norm_grad(values, norm_gain, norm_bias, upstream):
    unused, pull = jax.vjp(layer_norm, values, norm_gain, norm_bias)
    return pull(upstream)


def gather_rows(values):
    return lax.all_gather(values, "mp", axis=0, tiled=True)


def reduce_rows(values):
    return lax.psum_scatter(values, "mp", scatter_dimension=0, tiled=True)


def spread_rows(values):
    return lax.all_gather(values, "mp", axis=0, tiled=True)


def collect_rows(values):
    return lax.psum_scatter(values, "mp", scatter_dimension=0, tiled=True)


def fetch_weights(
    in_proj, out_proj, up_proj, down_proj, patch_embed, class_head, pos_table, norm_params
):
    small = (
        lax.all_gather(patch_embed, "dp", axis=0, tiled=True),
        lax.all_gather(class_head, "dp", axis=0, tiled=True),
        lax.all_gather(pos_table, "dp", axis=0, tiled=True),
        lax.all_gather(norm_params, "dp", axis=0, tiled=True),
    )
    gathered = (
        lax.all_gather(in_proj.astype(BF), "dp", axis=2, tiled=True),
        lax.all_gather(out_proj.astype(BF), "dp", axis=2, tiled=True),
        lax.all_gather(up_proj.astype(BF), "dp", axis=2, tiled=True),
        lax.all_gather(down_proj.astype(BF), "dp", axis=2, tiled=True),
    )
    mp_size = lax.axis_size("mp")
    owned = gathered[0].shape[0]
    width = gathered[0].shape[1]
    hidden = gathered[2].shape[2]
    local_d = width // mp_size
    local_f = hidden // mp_size
    swapped = (
        lax.all_to_all(
            gathered[0].reshape(owned, width * 3, mp_size, local_d),
            "mp",
            split_axis=2,
            concat_axis=0,
            tiled=True,
        ),
        lax.all_to_all(
            gathered[1].reshape(owned, 1, mp_size, local_d * width),
            "mp",
            split_axis=2,
            concat_axis=0,
            tiled=True,
        ),
        lax.all_to_all(
            gathered[2].reshape(owned, width, mp_size, local_f),
            "mp",
            split_axis=2,
            concat_axis=0,
            tiled=True,
        ),
        lax.all_to_all(
            gathered[3].reshape(owned, width, mp_size, local_f),
            "mp",
            split_axis=2,
            concat_axis=0,
            tiled=True,
        ),
    )
    layers = owned * mp_size
    return (
        swapped[0].reshape(layers, width, 3, local_d),
        swapped[1].reshape(layers, local_d, width),
        swapped[2].reshape(layers, width, local_f),
        swapped[3].reshape(layers, width, local_f),
        small[0].astype(BF),
        small[1].astype(BF),
        small[2],
        small[3],
    )


def attention_probs(joined, log_total):
    scores = jnp.einsum(
        "ithe,ishe->ihts", joined[:, :, 0], joined[:, :, 1], preferred_element_type=FL
    ) * HEAD_DIM ** (-0.5)
    return jnp.exp(scores - log_total)


def layer_forward(resid, weights, gains):
    w_qkv, w_out, w_up, w_down = weights
    gain_one, bias_one, gain_two, bias_two = gains
    head_count = w_qkv.shape[2] // HEAD_DIM
    rows_a = gather_rows(layer_norm(resid, gain_one, bias_one).astype(BF))
    image_count, tokens = (rows_a.shape[0], rows_a.shape[1])
    joined = jnp.einsum("itd,dce->itce", rows_a, w_qkv, preferred_element_type=FL).astype(BF)
    joined = joined.reshape(image_count, tokens, 3, head_count, HEAD_DIM)
    scores = jnp.einsum(
        "ithe,ishe->ihts", joined[:, :, 0], joined[:, :, 1], preferred_element_type=FL
    ) * HEAD_DIM ** (-0.5)
    row_max = jnp.max(scores, -1, keepdims=True)
    log_total = row_max + jnp.log(jnp.sum(jnp.exp(scores - row_max), -1, keepdims=True))
    probs = jnp.exp(scores - log_total).astype(BF)
    attended = jnp.einsum(
        "ihts,ishe->ithe", probs, joined[:, :, 2], preferred_element_type=FL
    ).astype(BF)
    attended = attended.reshape(image_count, tokens, head_count * HEAD_DIM)
    resid_mid = resid + reduce_rows(
        jnp.einsum("ite,ed->itd", attended, w_out, preferred_element_type=FL)
    )
    rows_b = gather_rows(layer_norm(resid_mid, gain_two, bias_two).astype(BF))
    pre_act = jnp.einsum("itd,df->itf", rows_b, w_up, preferred_element_type=FL)
    active = jax.nn.gelu(pre_act, approximate=False).astype(BF)
    resid_out = resid_mid + reduce_rows(
        jnp.einsum("itf,df->itd", active, w_down, preferred_element_type=FL)
    )
    return (resid_out, (resid, rows_a, joined, log_total, attended, resid_mid, rows_b, pre_act))


def layer_backward(grad_out, weights, gains, saved):
    w_qkv, w_out, w_up, w_down = weights
    gain_one, bias_one, gain_two, bias_two = gains
    resid, rows_a, joined, log_total, attended, resid_mid, rows_b, pre_act = saved
    image_count, tokens, head_count = (joined.shape[0], joined.shape[1], joined.shape[3])
    up_grad = spread_rows(grad_out.astype(BF))
    active = jax.nn.gelu(pre_act, approximate=False).astype(BF)
    d_down = jnp.einsum("itd,itf->df", up_grad, active, preferred_element_type=FL)
    d_active = jnp.einsum("itd,df->itf", up_grad, w_down, preferred_element_type=FL)
    unused, gelu_pull = jax.vjp(partial(jax.nn.gelu, approximate=False), pre_act)
    d_pre = gelu_pull(d_active)[0].astype(BF)
    d_up = jnp.einsum("itd,itf->df", rows_b, d_pre, preferred_element_type=FL)
    d_rows_b = collect_rows(jnp.einsum("itf,df->itd", d_pre, w_up, preferred_element_type=FL))
    d_mid, d_gain_two, d_bias_two = norm_grad(resid_mid, gain_two, bias_two, d_rows_b)
    d_mid = d_mid + grad_out
    mid_grad = spread_rows(d_mid.astype(BF))
    d_out = jnp.einsum("ite,itd->ed", attended, mid_grad, preferred_element_type=FL)
    d_att = jnp.einsum("itd,ed->ite", mid_grad, w_out, preferred_element_type=FL).astype(BF)
    d_att = d_att.reshape(image_count, tokens, head_count, HEAD_DIM)
    probs = attention_probs(joined, log_total)
    d_probs = jnp.einsum("ithe,ishe->ihts", d_att, joined[:, :, 2], preferred_element_type=FL)
    d_scores = (probs * (d_probs - jnp.sum(d_probs * probs, -1, keepdims=True))).astype(BF)
    d_value = jnp.einsum("ihts,ithe->ishe", probs.astype(BF), d_att, preferred_element_type=FL)
    d_query = jnp.einsum(
        "ihts,ishe->ithe", d_scores, joined[:, :, 1], preferred_element_type=FL
    ) * HEAD_DIM ** (-0.5)
    d_keys = jnp.einsum(
        "ihts,ithe->ishe", d_scores, joined[:, :, 0], preferred_element_type=FL
    ) * HEAD_DIM ** (-0.5)
    d_joined = (
        jnp.stack([d_query, d_keys, d_value], 2)
        .astype(BF)
        .reshape(image_count, tokens, 3, head_count * HEAD_DIM)
    )
    d_qkv = jnp.einsum("itd,itce->dce", rows_a, d_joined, preferred_element_type=FL)
    d_rows_a = collect_rows(jnp.einsum("itce,dce->itd", d_joined, w_qkv, preferred_element_type=FL))
    d_resid, d_gain_one, d_bias_one = norm_grad(resid, gain_one, bias_one, d_rows_a)
    return (
        d_resid + d_mid,
        (d_qkv, d_out, d_up, d_down),
        [d_gain_one, d_bias_one, d_gain_two, d_bias_two],
    )


def forward_stack(images, fetched):
    w_qkv, w_out, w_up, w_down, patch_bf, head_bf, pos_full, norm_full = fetched
    layers = w_qkv.shape[0]
    embedded = jnp.einsum("ipc,cd->ipd", images, patch_bf, preferred_element_type=FL)
    first_row = jnp.zeros((images.shape[0], 1, embedded.shape[2]), FL)
    resid = jnp.concatenate([first_row, embedded], 1) + pos_full.T[None]
    saved_all = []
    gain_sets = []
    for layer_num in range(layers):
        gains = tuple((norm_full[:, 4 * layer_num + column] for column in range(4)))
        layer_w = (w_qkv[layer_num], w_out[layer_num], w_up[layer_num], w_down[layer_num])
        resid, saved = layer_forward(resid, layer_w, gains)
        saved_all.append(saved)
        gain_sets.append(gains)
    final_in = resid[:, 0]
    gain_final = norm_full[:, 4 * layers]
    bias_final = norm_full[:, 4 * layers + 1]
    features = layer_norm(final_in, gain_final, bias_final).astype(BF)
    logits = jnp.dot(features, head_bf, preferred_element_type=FL)
    row_max = jnp.max(logits, -1, keepdims=True)
    log_total = row_max + jnp.log(jnp.sum(jnp.exp(logits - row_max), -1, keepdims=True))
    return (resid, saved_all, gain_sets, final_in, features, logits, log_total)


def local_gram(matrix):
    return jnp.einsum("lde,lfe->ldf", matrix, matrix, precision=PRECISE)


def newton_schulz(currents, grams, renew):
    sizes = [jnp.sqrt(jnp.einsum("ldd->l", gram_mat))[:, None, None] + 1e-07 for gram_mat in grams]
    currents = [currents[index] / sizes[index] for index in range(4)]
    grams = [grams[index] / (sizes[index] * sizes[index]) for index in range(4)]
    for turn in range(5):
        for index in range(4):
            mixed = NS_B * grams[index] + NS_C * jnp.einsum(
                "lde,lef->ldf", grams[index], grams[index], precision=PRECISE
            )
            currents[index] = NS_A * currents[index] + jnp.einsum(
                "lde,lef->ldf", mixed, currents[index], precision=PRECISE
            )
        if turn < 4:
            grams = renew(currents)
    return currents


def body(
    pool_images,
    pick_rows,
    pick_weight,
    pick_label,
    in_proj,
    out_proj,
    up_proj,
    down_proj,
    in_moment,
    out_moment,
    up_moment,
    down_moment,
    patch_embed,
    class_head,
    pos_table,
    norm_params,
    patch_first,
    head_first,
    pos_first,
    norm_first,
    patch_second,
    head_second,
    pos_second,
    norm_second,
):
    mp_size = lax.axis_size("mp")
    mp_index = lax.axis_index("mp")
    per_batch = pick_rows.shape[0] // MB
    per_core = per_batch // mp_size
    own_mults = lax.dynamic_slice_in_dim(pick_weight.reshape(MB, mp_size, per_core), mp_index, 1, 1)
    weight_local = jnp.sum(own_mults.astype(FL))
    weight_early = lax.psum(weight_local, ("dp", "mp"))
    masters = (
        in_proj,
        out_proj,
        up_proj,
        down_proj,
        patch_embed,
        class_head,
        pos_table,
        norm_params,
    )
    loss_local = jnp.zeros((), FL)
    muon_acc = None
    adam_acc = None
    pool_score = None
    for micro_idx in range(MB):
        fetched = fetch_weights(*masters)
        w_qkv, w_out, w_up, w_down, patch_bf, head_bf, pos_full, norm_full = fetched
        layers = w_qkv.shape[0]
        if micro_idx == 0:
            half = pool_images.shape[0] // mp_size
            pool_part = lax.dynamic_slice_in_dim(pool_images, mp_index * half, half)
            pool_out = forward_stack(pool_part, fetched)
            pool_score = pool_out[6][:, 0] - jnp.mean(pool_out[5], -1)
        offset = micro_idx * per_batch + mp_index * per_core
        chosen = lax.dynamic_slice_in_dim(pick_rows, offset, per_core)
        targets = lax.dynamic_slice_in_dim(pick_label, offset, per_core)
        weights = lax.dynamic_slice_in_dim(pick_weight, offset, per_core).astype(FL)
        images = pool_images[chosen]
        resid, saved_all, gain_sets, final_in, features, logits, log_total = forward_stack(
            images, fetched
        )
        gain_final = norm_full[:, 4 * layers]
        bias_final = norm_full[:, 4 * layers + 1]
        is_target = jnp.arange(logits.shape[1], dtype=jnp.int32)[None] == targets[:, None]
        target_logit = jnp.sum(jnp.where(is_target, logits, 0.0), -1)
        loss_local = loss_local + jnp.sum(weights * (log_total[:, 0] - target_logit))
        d_logits = (weights[:, None] * (jnp.exp(logits - log_total) - is_target.astype(FL))).astype(
            BF
        )
        d_head = jnp.einsum("ic,id->cd", features, d_logits, preferred_element_type=FL)
        d_features = jnp.einsum("id,cd->ic", d_logits, head_bf, preferred_element_type=FL)
        d_final, d_gain_final, d_bias_final = norm_grad(
            final_in, gain_final, bias_final, d_features
        )
        grad_resid = jnp.zeros_like(resid).at[:, 0].set(d_final)
        mat_grads = [None] * layers
        norm_cols = [None] * layers
        for layer_num in reversed(range(layers)):
            layer_w = (w_qkv[layer_num], w_out[layer_num], w_up[layer_num], w_down[layer_num])
            grad_resid, mat_grads[layer_num], norm_cols[layer_num] = layer_backward(
                grad_resid, layer_w, gain_sets[layer_num], saved_all[layer_num]
            )
        d_patch = jnp.einsum(
            "ipc,ipd->cd", images, grad_resid[:, 1:].astype(BF), preferred_element_type=FL
        )
        d_pos = jnp.sum(grad_resid, 0).T
        columns = [column for group in norm_cols for column in group] + [d_gain_final, d_bias_final]
        d_norm = jnp.stack(columns, 1)
        width = w_qkv.shape[1]
        local_d = w_qkv.shape[3]
        local_f = w_up.shape[2]
        stacked = [jnp.stack([grads[index] for grads in mat_grads], 0) for index in range(4)]
        swapped = (
            lax.all_to_all(
                stacked[0].reshape(layers, width * 3, 1, local_d),
                "mp",
                split_axis=0,
                concat_axis=2,
                tiled=True,
            ),
            lax.all_to_all(
                stacked[1].reshape(layers, 1, 1, local_d * width),
                "mp",
                split_axis=0,
                concat_axis=2,
                tiled=True,
            ),
            lax.all_to_all(
                stacked[2].reshape(layers, width, 1, local_f),
                "mp",
                split_axis=0,
                concat_axis=2,
                tiled=True,
            ),
            lax.all_to_all(
                stacked[3].reshape(layers, width, 1, local_f),
                "mp",
                split_axis=0,
                concat_axis=2,
                tiled=True,
            ),
        )
        owned = layers // mp_size
        reduced = (
            lax.psum_scatter(
                swapped[0].reshape(owned, width, 3 * width), "dp", scatter_dimension=2, tiled=True
            ),
            lax.psum_scatter(
                swapped[1].reshape(owned, width, width), "dp", scatter_dimension=2, tiled=True
            ),
            lax.psum_scatter(
                swapped[2].reshape(owned, width, local_f * mp_size),
                "dp",
                scatter_dimension=2,
                tiled=True,
            ),
            lax.psum_scatter(
                swapped[3].reshape(owned, width, local_f * mp_size),
                "dp",
                scatter_dimension=2,
                tiled=True,
            ),
        )
        small = (
            lax.psum_scatter(d_patch, "dp", scatter_dimension=0, tiled=True),
            lax.psum_scatter(d_head, "dp", scatter_dimension=0, tiled=True),
            lax.psum_scatter(d_pos, "dp", scatter_dimension=0, tiled=True),
            lax.psum_scatter(d_norm, "dp", scatter_dimension=0, tiled=True),
        )
        if muon_acc is None:
            muon_acc = list(reduced)
            adam_acc = list(small)
        else:
            muon_acc = [total + part for total, part in zip(muon_acc, reduced)]
            adam_acc = [total + part for total, part in zip(adam_acc, small)]
    adam_raw = lax.psum((adam_acc[0], adam_acc[1], adam_acc[2], adam_acc[3]), "mp")
    squares = sum([jnp.sum(grad * grad) for grad in muon_acc]) + 0.5 * sum(
        [jnp.sum(grad * grad) for grad in adam_raw]
    )
    extra = jnp.zeros((), FL)
    summed = lax.psum((loss_local, squares, extra), ("dp", "mp"))
    grad_norm = jnp.sqrt(summed[1]) / weight_early
    scaling = THRESHOLD / jnp.maximum(grad_norm, THRESHOLD) / weight_early
    moments = (in_moment, out_moment, up_moment, down_moment)
    new_moms = [MOMENTUM * moments[index] + muon_acc[index] * scaling for index in range(4)]
    dp_size = lax.axis_size("dp")
    full_moms = (
        lax.all_gather(new_moms[0], "dp", axis=2, tiled=True),
        lax.all_gather(new_moms[1], "dp", axis=2, tiled=True),
        lax.all_gather(new_moms[2], "dp", axis=2, tiled=True),
        lax.all_gather(new_moms[3], "dp", axis=2, tiled=True),
    )
    full_moms = list(full_moms)
    wholes = newton_schulz(
        full_moms,
        [local_gram(mat) for mat in full_moms],
        lambda mats: [local_gram(mat) for mat in mats],
    )
    dp_index = lax.axis_index("dp")
    currents = [
        lax.dynamic_slice_in_dim(
            wholes[index], dp_index * new_moms[index].shape[2], new_moms[index].shape[2], 2
        )
        for index in range(4)
    ]
    new_mats = []
    for index in range(4):
        weight = masters[index]
        rate = MUON_RATES[index]
        factor = 0.2 * math.sqrt(max(weight.shape[1], weight.shape[2] * dp_size))
        new_mats.append(weight * (1.0 - rate * DECAY) - rate * factor * currents[index])
    firsts = (patch_first, head_first, pos_first, norm_first)
    seconds = (patch_second, head_second, pos_second, norm_second)
    new_ws, new_fs, new_ss = ([], [], [])
    for index in range(4):
        grad = adam_raw[index] * scaling
        rate = ADAM_RATES[index]
        first = BETA_ONE * firsts[index] + (1.0 - BETA_ONE) * grad
        second = BETA_TWO * seconds[index] + (1.0 - BETA_TWO) * grad * grad
        step_size = (
            first / (1.0 - BETA_ONE**STEP) / (jnp.sqrt(second / (1.0 - BETA_TWO**STEP)) + ADAM_EPS)
        )
        new_ws.append(masters[4 + index] * (1.0 - rate * DECAY) - rate * step_size)
        new_fs.append(first)
        new_ss.append(second)
    return (
        summed[0],
        weight_early,
        grad_norm,
        pool_score,
        new_mats[0],
        new_mats[1],
        new_mats[2],
        new_mats[3],
        new_moms[0],
        new_moms[1],
        new_moms[2],
        new_moms[3],
        new_ws[0],
        new_ws[1],
        new_ws[2],
        new_ws[3],
        new_fs[0],
        new_fs[1],
        new_fs[2],
        new_fs[3],
        new_ss[0],
        new_ss[1],
        new_ss[2],
        new_ss[3],
    )


def solution(mesh):
    in_specs = (
        P("dp", None, None),
        P("dp"),
        P("dp"),
        P("dp"),
        P("mp", None, "dp"),
        P("mp", None, "dp"),
        P("mp", None, "dp"),
        P("mp", None, "dp"),
        P("mp", None, "dp"),
        P("mp", None, "dp"),
        P("mp", None, "dp"),
        P("mp", None, "dp"),
        P("dp", None),
        P("dp", None),
        P("dp", None),
        P("dp", None),
        P("dp", None),
        P("dp", None),
        P("dp", None),
        P("dp", None),
        P("dp", None),
        P("dp", None),
        P("dp", None),
        P("dp", None),
    )
    out_specs = (
        P(),
        P(),
        P(),
        P(("dp", "mp")),
        P("mp", None, "dp"),
        P("mp", None, "dp"),
        P("mp", None, "dp"),
        P("mp", None, "dp"),
        P("mp", None, "dp"),
        P("mp", None, "dp"),
        P("mp", None, "dp"),
        P("mp", None, "dp"),
        P("dp", None),
        P("dp", None),
        P("dp", None),
        P("dp", None),
        P("dp", None),
        P("dp", None),
        P("dp", None),
        P("dp", None),
        P("dp", None),
        P("dp", None),
        P("dp", None),
        P("dp", None),
    )
    return jax.shard_map(body, mesh=mesh, in_specs=in_specs, out_specs=out_specs, check_vma=False)
```

profile of v0, /device:TPU:0, one launch (start us, length us, event | category | flops | bytes accessed | tf_op | source)
XLA Modules:
  0.0 1955.6 jit_solution(17691073928941042338)
XLA Ops:
  9.1 47.6 %all_gather.108 = bf16[1,384,1152]{1,2,0:T(8,128)(2,1)S(1)} all-gather(bf16[1,384,72]{1,2,0:T(8,128)(2,1)S(1)} %convert_element_type.257), channel_id=1, replica_groups=mesh['dp'=16,'mp'=2] {'dp'}, dimensions={2}, use_global_device_ids=true | all-gather | bytes 940032 | tf_op jit(solution)/shard_map/all_gather | solution.py:69
  71.0 37.6 %all_gather.105 = f32[384,197]{1,0:T(8,128)S(1)} all-gather(f32[24,197]{1,0:T(8,128)S(1)} %copy-done.199), channel_id=1, replica_groups=mesh['dp'=16,'mp'=2] {'dp'}, dimensions={0}, use_global_device_ids=true | all-gather | bytes 321504 | tf_op jit(solution)/shard_map/all_gather | solution.py:65
  108.8 40.9 %all_gather.104 = bf16[768,384]{1,0:T(8,128)(2,1)S(1)} all-gather(bf16[48,384]{1,0:T(8,128)(2,1)S(1)} %convert.308), channel_id=1, replica_groups=mesh['dp'=16,'mp'=2] {'dp'}, dimensions={0}, use_global_device_ids=true | all-gather | bytes 626688 | tf_op jit(solution)/shard_map/all_gather | solution.py:63
  149.8 5.9 gather_fusion.1
  161.4 36.7 %all-gather = f32[16,24,10]{1,2,0:T(8,128)S(1)} all-gather(f32[1,24,10]{1,2,0:T(8,128)S(1)} %bitcast.890), channel_id=1, replica_groups=mesh['dp'=16,'mp'=2] {'dp'}, dimensions={0}, use_global_device_ids=true | all-gather | bytes 16320 | tf_op jit(solution)/shard_map/all_gather | solution.py:66
  198.9 5.2 gather_fusion
  217.8 41.3 %all_gather.109 = bf16[1,384,384]{1,2,0:T(8,128)(2,1)} all-gather(bf16[1,384,24]{1,2,0:T(8,128)(2,1)S(1)} %convert_element_type.262), channel_id=1, replica_groups=mesh['dp'=16,'mp'=2] {'dp'}, dimensions={2}, use_global_device_ids=true | all-gather | bytes 313344 | tf_op jit(solution)/shard_map/all_gather | solution.py:70
  320.3 33.0 %all-gather.11.cloned.1.call-done = bf16[1,384,1536]{1,2,0:T(8,128)(2,1)} async-done(((bf16[1,384,96]{1,2,0:T(8,128)(2,1)}), bf16[1,384,1536]{1,2,0:T(8,128)(2,1)}) %all-gather.11.cloned.1.call-update) | async-done | bytes 1179664 | tf_op jit(solution)/shard_map/all_gather | solution.py:71
  360.1 51.8 %all-gather.13.cloned.1.call-done = bf16[1,384,1536]{1,2,0:T(8,128)(2,1)} async-done(((bf16[1,384,96]{1,2,0:T(8,128)(2,1)}), bf16[1,384,1536]{1,2,0:T(8,128)(2,1)}) %all-gather.13.cloned.1.call-update) | async-done | bytes 1179664 | tf_op jit(solution)/shard_map/all_gather | solution.py:72
  433.8 6.7 multiply_convert_fusion.5
  449.2 6.5 multiply_convert_fusion.7
  509.1 6.4 all-reduce.45.cloned.1.call-done
  547.6 6.5 multiply_convert_fusion.4
  567.3 7.7 multiply_convert_fusion.6
  580.7 48.0 %all_gather.115 = bf16[384,1000]{1,0:T(8,128)(2,1)} all-gather(bf16[24,1000]{1,0:T(8,128)(2,1)S(1)} %convert.309), channel_id=1, replica_groups=mesh['dp'=16,'mp'=2] {'dp'}, dimensions={0}, use_global_device_ids=true | all-gather | bytes 816000 | tf_op jit(solution)/shard_map/all_gather | solution.py:64
  664.2 6.9 fusion.156
  671.1 10.7 all-reduce.59.cloned.1.call-done
  681.8 8.2 multiply_reduce_fusion.14
  698.6 6.9 fusion.406
  725.4 14.4 fusion.62
  740.1 8.5 all-reduce.57.cloned.1.call-done
  748.6 7.8 multiply_reduce_fusion.15
  758.2 6.9 fusion.404
  789.2 18.3 all-reduce.55.cloned.1.call-done
  807.5 8.0 multiply_reduce_fusion.16
  818.3 6.9 fusion.401
  895.0 7.3 multiply_reduce_fusion.21
  904.1 6.9 fusion.398
  960.8 8.2 copy.852
  970.6 5.0 all-to-all-start.10
  993.6 8.2 copy.857
  1029.9 111.3 %reduce-scatter.47.cloned.1.call-done = f32[48,384]{1,0:T(8,128)} async-done(((f32[768,384]{1,0:T(8,128)}), f32[48,384]{1,0:T(8,128)}) %reduce-scatter.47.cloned.1.call-update) | async-done | bytes 73744 | tf_op jit(solution)/shard_map/reduce_scatter | solution.py:396
  1141.3 5.2 all_to_all.186
  1162.0 13.7 fusion.60
  1181.1 98.0 %reduce-scatter.53.cloned.1.call-done = f32[1,384,24]{1,2,0:T(8,128)} async-done(((f32[1,384,384]{1,2,0:T(8,128)}), f32[1,384,24]{1,2,0:T(8,128)}) %reduce-scatter.53.cloned.1.call-update) | async-done | bytes 36880
  1280.7 74.9 %all-reduce.21 = f32[384,10]{0,1:T(8,128)S(1)} all-reduce(f32[384,10]{0,1:T(8,128)S(1)} %add.1007), channel_id=33, replica_groups=mesh['dp'=16,'mp'=2] {'dp'}, use_global_device_ids=true, to_apply=%region_115.116.clone | all-reduce | flops 3840 | bytes 30720
  1355.7 49.5 %reduce-scatter.51.cloned.1.call-done = f32[24,197]{1,0:T(8,128)} async-done(((f32[384,197]{1,0:T(8,128)}), f32[24,197]{1,0:T(8,128)}) %reduce-scatter.51.cloned.1.call-update) | async-done | bytes 18928 | tf_op jit(solution)/shard_map/reduce_scatter | solution.py:398
  1410.5 14.2 all-reduce.51.cloned.1.call-done
  1430.3 219.1 %all-reduce.49.cloned.1.call-done = (f32[1,384,1152]{1,0,2:T(1,128)}, f32[1,384,1536]{1,0,2:T(1,128)}, f32[1,384,1536]{1,0,2:T(1,128)}) async-done(((f32[1,384,1152]{1,0,2:T(1,128)}, f32[1,384,1536]{1,0,2:T(1,128)}, f32[1,384,1536]{1,0,2:T(1,128)}), (f32[1,384,1152]{1,0,2:T(1,128)}, f32[1,384,1536]{1,0,2:T(1,128)}, f32[1,384,1536]{1,0,2:T(1,128)})) %all-reduce.49.cloned.1.call-update) | async-done | bytes 6488080
  1655.8 39.5 %all-reduce.22 = (f32[]{:T(128)}, f32[]{:T(128)}, f32[]{:T(128)}) all-reduce(f32[]{:T(128)S(6)} %add.883, f32[]{:T(128)} %fusion.295, f32[]{:T(128)S(6)} %add.907), channel_id=1, replica_groups=mesh['dp'=16,'mp'=2] {'dp','mp'}, use_global_device_ids=true, to_apply=%region_44.45 | all-reduce | flops 3 | bytes 24 | tf_op jit(solution)/shard_map/psum | solution.py:412
  1702.9 44.4 %all_gather.133 = f32[1,384,384]{1,2,0:T(8,128)S(1)} all-gather(f32[1,384,24]{1,2,0:T(8,128)S(1)} %multiply_add_fusion.2), channel_id=1, replica_groups=mesh['dp'=16,'mp'=2] {'dp'}, dimensions={2}, use_global_device_ids=true | all-gather | bytes 626688 | tf_op jit(solution)/shard_map/all_gather | solution.py:420
  1776.0 6.5 select_reduce_fusion.3
  1825.0 7.3 select_reduce_fusion.1
  1834.5 5.2 copy.894
  1839.7 6.3 fusion.22
  1887.2 6.9 select_reduce_fusion
  1896.2 5.4 copy.898
  1901.6 6.3 fusion.26
  (1165 shorter events, 684.8 us)
Async XLA Ops:
  66.6 202.9 %all-to-all-start = ((bf16[1,1152,2,192]{1,3,0,2:T(8,128)(2,1)}), bf16[1,1152,2,192]{1,3,0,2:T(8,128)(2,1)}, u32[]{:S(2)}, u32[]{:S(2)}) async-start(bf16[1,1152,2,192]{1,3,0,2:T(8,128)(2,1)} %copy.711), calls=%async_computation | async-start | bytes 1769472 | tf_op jit(solution)/shard_map/all_to_all | solution.py:81
  269.5 18.5 all-to-all-start.1
  273.7 39.2 %all-reduce.41.cloned.1.call-start = ((), (), s32[]{:S(2)}) async-start(), calls=%async_computation.44 | async-start | bytes 2420736
  296.6 56.6 %all-gather.11.cloned.1.call-start = ((), (), s32[]{:S(2)}) async-start(), calls=%async_computation.25 | async-start | bytes 1253376 | tf_op jit(solution)/shard_map/all_gather | solution.py:71
  298.3 113.6 %all-gather.13.cloned.1.call-start = ((), (), s32[]{:S(2)}) async-start(), calls=%async_computation.26 | async-start | bytes 1253376 | tf_op jit(solution)/shard_map/all_gather | solution.py:72
  299.9 114.3 %reduce-scatter.31.cloned.1.call-start = ((), (), s32[]{:S(2)}) async-start(), calls=%async_computation.24 | async-start | bytes 1843200 | tf_op jit(solution)/shard_map/reduce_scatter | solution.py:48
  355.6 69.4 %all-to-all-start.2 = ((bf16[1,384,2,768]{3,1,0,2:T(8,128)(2,1)}), bf16[1,384,2,768]{3,1,0,2:T(8,128)(2,1)}, u32[]{:S(2)}, u32[]{:S(2)}) async-start(bf16[1,384,2,768]{3,1,0,2:T(8,128)(2,1)} %copy.725), calls=%async_computation.3 | async-start | bytes 2359296 | tf_op jit(solution)/shard_map/all_to_all | solution.py:95
  425.1 15.4 all-to-all-start.3
  429.6 37.7 %all-reduce.43.cloned.1.call-start = ((), (), s32[]{:S(2)}) async-start(), calls=%async_computation.45 | async-start | bytes 2420736
  444.2 31.0 %reduce-scatter.33.cloned.1.call-start = ((), (), s32[]{:S(2)}) async-start(), calls=%async_computation.27 | async-start | bytes 1843200 | tf_op jit(solution)/shard_map/reduce_scatter | solution.py:48
  459.7 41.4 %all-gather.15.cloned.1.call-start = ((), (), s32[]{:S(2)}) async-start(), calls=%async_computation.30 | async-start | bytes 1843200 | tf_op jit(solution)/shard_map/all_gather | solution.py:44
  463.8 51.6 %all-reduce.45.cloned.1.call-start = ((), (), s32[]{:S(2)}) async-start(), calls=%async_computation.46 | async-start | bytes 2420736
  494.3 33.4 %reduce-scatter.35.cloned.1.call-start = ((), (), s32[]{:S(2)}) async-start(), calls=%async_computation.28 | async-start | bytes 1843200 | tf_op jit(solution)/shard_map/reduce_scatter | solution.py:48
  500.7 127.9 %reduce-scatter.39.cloned.1.call-start = ((), (), s32[]{:S(2)}) async-start(), calls=%async_computation.31 | async-start | bytes 3686400 | tf_op jit(solution)/shard_map/reduce_scatter | solution.py:48
  509.1 124.5 %all-reduce.47.cloned.1.call-start = ((), (), s32[]{:S(2)}) async-start(), calls=%async_computation.47 | async-start | bytes 2420736
  567.2 68.1 %reduce-scatter.37.cloned.1.call-start = ((), (), s32[]{:S(2)}) async-start(), calls=%async_computation.29 | async-start | bytes 1843200 | tf_op jit(solution)/shard_map/reduce_scatter | solution.py:48
  579.1 85.1 %all-gather.17.cloned.1.call-start = ((), (), s32[]{:S(2)}) async-start(), calls=%async_computation.32 | async-start | bytes 1843200 | tf_op jit(solution)/shard_map/all_gather | solution.py:44
  633.5 48.3 %all-reduce.59.cloned.1.call-start = ((), (), s32[]{:S(2)}) async-start(), calls=%async_computation.54 | async-start | bytes 4841472
  663.9 84.6 %all-reduce.57.cloned.1.call-start = ((), (), s32[]{:S(2)}) async-start(), calls=%async_computation.53 | async-start | bytes 4841472
  725.3 60.4 %reduce-scatter.41.cloned.1.call-start = ((), (), s32[]{:S(2)}) async-start(), calls=%async_computation.33 | async-start | bytes 3686400 | tf_op jit(solution)/shard_map/reduce_scatter | solution.py:48
  739.8 67.6 %all-reduce.55.cloned.1.call-start = ((), (), s32[]{:S(2)}) async-start(), calls=%async_computation.52 | async-start | bytes 4841472
  784.3 62.1 %all-gather.19.cloned.1.call-start = ((), (), s32[]{:S(2)}) async-start(), calls=%async_computation.34 | async-start | bytes 1843200 | tf_op jit(solution)/shard_map/all_gather | solution.py:44
  788.9 106.1 %all-reduce.53.cloned.1.call-start = ((), (), s32[]{:S(2)}) async-start(), calls=%async_computation.51 | async-start | bytes 4841472
  845.9 80.5 %reduce-scatter.43.cloned.1.call-start = ((), (), s32[]{:S(2)}) async-start(), calls=%async_computation.35 | async-start | bytes 3686400 | tf_op jit(solution)/shard_map/reduce_scatter | solution.py:48
  854.2 175.7 %reduce-scatter.49.cloned.1.call-start = ((), (), s32[]{:S(2)}) async-start(), calls=%async_computation.42 | async-start | bytes 1671168 | tf_op jit(solution)/shard_map/reduce_scatter | solution.py:397
  865.6 275.6 %reduce-scatter.47.cloned.1.call-start = ((), (), s32[]{:S(2)}) async-start(), calls=%async_computation.41 | async-start | bytes 1253376 | tf_op jit(solution)/shard_map/reduce_scatter | solution.py:396
  919.4 10.6 all-to-all-start.6
  923.0 235.0 %all-gather.21.cloned.1.call-start = ((), (), s32[]{:S(2)}) async-start(), calls=%async_computation.36 | async-start | bytes 1843200 | tf_op jit(solution)/shard_map/all_gather | solution.py:44
  934.2 12.7 all-to-all-start.8
  939.1 340.0 %reduce-scatter.53.cloned.1.call-start = ((), (), s32[]{:S(2)}) async-start(), calls=%async_computation.48 | async-start | bytes 626688
  947.0 8.1 all-to-all-start.9
  970.6 8.6 all-to-all-start.10
  979.2 8.6 all-to-all-start.11
  984.2 421.1 %reduce-scatter.51.cloned.1.call-start = ((), (), s32[]{:S(2)}) async-start(), calls=%async_computation.43 | async-start | bytes 417792 | tf_op jit(solution)/shard_map/reduce_scatter | solution.py:398
  1014.7 126.6 %all-to-all-start.4 = ((f32[2,1152,1,192]{1,3,2,0:T(8,128)}), f32[2,1152,1,192]{1,3,2,0:T(8,128)}, u32[]{:S(2)}, u32[]{:S(2)}) async-start(f32[2,1152,1,192]{1,3,2,0:T(8,128)} %copy.811), calls=%async_computation.8 | async-start | bytes 3538944 | tf_op jit(solution)/shard_map/all_to_all | solution.py:345
  1019.6 405.1 %all-reduce.51.cloned.1.call-start = ((), (), s32[]{:S(2)}) async-start(), calls=%async_computation.50 | async-start | bytes 344064 | tf_op jit(solution)/shard_map/psum | solution.py:407
  1141.2 508.2 %all-reduce.49.cloned.1.call-start = ((), (), s32[]{:S(2)}) async-start(), calls=%async_computation.49 | async-start | bytes 12976128
  1157.7 616.0 %reduce-scatter.45.cloned.1.call-start = ((), (), s32[]{:S(2)}) async-start(), calls=%async_computation.37 | async-start | bytes 3686400 | tf_op jit(solution)/shard_map/reduce_scatter | solution.py:48
  1175.8 521.6 %copy-start.196 = (f32[1,384,72]{1,2,0:T(8,128)S(1)}, f32[1,384,72]{1,2,0:T(8,128)}, u32[]{:S(2)}) copy-start(f32[1,384,72]{1,2,0:T(8,128)} %param.36) | copy-start | bytes 331780
  1175.8 522.4 %copy-start.155 = (f32[1,384,72]{1,2,0:T(8,128)S(1)}, f32[1,384,72]{1,2,0:T(8,128)}, u32[]{:S(2)}) copy-start(f32[1,384,72]{1,2,0:T(8,128)} %param.32) | copy-start | bytes 331780
  1175.8 523.2 %copy-start.150 = (f32[1,384,96]{1,2,0:T(8,128)S(1)}, f32[1,384,96]{1,2,0:T(8,128)}, u32[]{:S(2)}) copy-start(f32[1,384,96]{1,2,0:T(8,128)} %param.34) | copy-start | bytes 442372
  1175.8 524.0 %copy-start.151 = (f32[1,384,96]{1,2,0:T(8,128)S(1)}, f32[1,384,96]{1,2,0:T(8,128)}, u32[]{:S(2)}) copy-start(f32[1,384,96]{1,2,0:T(8,128)} %param.35) | copy-start | bytes 442372
  1175.8 524.9 %copy-start.194 = (f32[1,384,96]{1,2,0:T(8,128)S(1)}, f32[1,384,96]{1,2,0:T(8,128)}, u32[]{:S(2)}) copy-start(f32[1,384,96]{1,2,0:T(8,128)} %param.38) | copy-start | bytes 442372
  1175.9 526.4 %copy-start.209 = (f32[1,384,24]{1,2,0:T(8,128)S(1)}, f32[1,384,24]{1,2,0:T(8,128)}, u32[]{:S(2)}) copy-start(f32[1,384,24]{1,2,0:T(8,128)} %param.37) | copy-start | bytes 110596
  1175.9 600.1 %all-gather.23.cloned.1.call-start = ((), (), s32[]{:S(2)}) async-start(), calls=%async_computation.38 | async-start | bytes 1880064 | tf_op jit(solution)/shard_map/all_gather | solution.py:419
  1279.1 423.2 %copy-start.191 = (f32[1,384,24]{1,2,0:T(8,128)S(1)}, f32[1,384,24]{1,2,0:T(8,128)}, u32[]{:S(2)}) copy-start(f32[1,384,24]{1,2,0:T(8,128)} %reduce-scatter.53.cloned.1.call-done) | copy-start | bytes 110596
  1698.2 126.8 %all-gather.25.cloned.1.call-start = ((), (), s32[]{:S(2)}) async-start(), calls=%async_computation.39 | async-start | bytes 2506752 | tf_op jit(solution)/shard_map/all_gather | solution.py:421
  1702.2 185.0 %all-gather.27.cloned.1.call-start = ((), (), s32[]{:S(2)}) async-start(), calls=%async_computation.40 | async-start | bytes 2506752 | tf_op jit(solution)/shard_map/all_gather | solution.py:422
  (279 other events, 3254.1 us)
Sparse Core Ops, SparseCore 0:
  296.8 16.0 all-reduce.40
  315.1 9.8 reduce-scatter.30
  444.3 18.6 all-reduce.42
  465.2 9.8 reduce-scatter.32
  476.5 10.4 all-gather.14
  494.4 21.0 all-reduce.44
  517.7 9.8 reduce-scatter.34
  530.0 11.2 reduce-scatter.38
  567.3 21.0 all-reduce.46
  590.7 9.8 reduce-scatter.36
  633.6 5.1 all-gather.16
  664.0 17.7 all-reduce.58
  725.5 23.0 all-reduce.56
  750.7 11.1 reduce-scatter.40
  784.4 23.0 all-reduce.54
  809.0 10.4 all-gather.18
  846.0 23.0 all-reduce.52
  871.2 11.1 reduce-scatter.42
  887.3 125.8 reduce-scatter.48
  1017.7 123.4 reduce-scatter.46
  1142.7 8.2 all-gather.20
  1155.7 123.3 reduce-scatter.52
  1284.5 120.7 reduce-scatter.50
  1407.5 17.1 all-reduce.50
  1431.1 218.2 all-reduce.48
  1651.6 8.9 reduce-scatter.44
Sparse Core Ops, SparseCore 1:
  300.9 52.3 all-gather.10
  356.9 54.9 all-gather.12
  1698.3 60.9 all-gather.22
  1762.6 60.9 all-gather.24
  1826.4 60.7 all-gather.26
where the time goes:
time: 1970 us; the launch traced here: 1960 us
  waiting for transfers between devices  634 us (32%)
  blocking collectives  462 us (23%)
  matrix products  341 us (17%)
  other arithmetic  219 us (11%)
  local copies, waits for them, and re-layouts  213 us (11%)
  starting transfers between devices  50 us (3%)
  between operations  36.2 us (2%)
    unnamed x41, waiting for transfers between devices  364 us
    reduce_scatter x1, waiting for transfers between devices, body(): lax.psum_scatter(d_patch, 'dp', scatter_dimension=0, tiled=True)  111 us
    unnamed x1, blocking collectives  74.9 us
    dot_general x20, matrix products, local_gram(): return jnp.einsum('lde,lfe->ldf', matrix, matrix, precision=PRECISE)  74.2 us
    dot_general x20, matrix products, newton_schulz(): jnp.einsum('lde,lef->ldf', mixed, currents[index], precision=PRECISE)  69.2 us
    all_gather x1, waiting for transfers between devices, fetch_weights(): lax.all_gather(down_proj.astype(BF), 'dp', axis=2, tiled=True)  51.8 us
    reduce_scatter x1, waiting for transfers between devices, body(): lax.psum_scatter(d_pos, 'dp', scatter_dimension=0, tiled=True)  49.5 us
    all_gather x1, blocking collectives, fetch_weights(): lax.all_gather(class_head, 'dp', axis=0, tiled=True)  48 us
  transfers between devices with their start and end apart: 41, of which 15 were waited for; matrix products, arithmetic and copies ran while one was open for 32% of the time, Pallas kernels for 0%

commit v1 on v0

v1 whole, which is shorter than its diff:
```python
import math

import jax
import jax.numpy as jnp
from jax import lax
from jax.experimental import pallas as pl
from jax.experimental.pallas import tpu as pltpu
from jax.sharding import PartitionSpec as P

HEAD_DIM = 64
STEP = 5
EPSILON = 1e-06
NS_A = 3.4445
NS_B = -4.775
NS_C = 2.0315
MOMENTUM = 0.95
MUON_RATES = (0.1, 0.4, 0.1, 0.1)
DECAY = 0.01
BETA_ONE = 0.9
BETA_TWO = 0.95
ADAM_EPS = 1e-08
ADAM_RATES = (0.01, 0.02, 0.1, 0.2)
THRESHOLD = 0.01
PRECISE = lax.Precision.HIGHEST
BF = jnp.bfloat16
FL = jnp.float32


def layer_norm(values, gain, bias):
    centered = values - jnp.mean(values, -1, keepdims=True)
    inverse = lax.rsqrt(jnp.mean(centered * centered, -1, keepdims=True) + EPSILON)
    unit = centered * inverse
    return (unit * gain + bias, unit, inverse)


def layer_norm_grad(upstream, unit, inverse, gain):
    axes = tuple(range(upstream.ndim - 1))
    d_gain = jnp.sum(upstream * unit, axes)
    d_bias = jnp.sum(upstream, axes)
    scaled = upstream * gain
    d_values = inverse * (
        scaled
        - jnp.mean(scaled, -1, keepdims=True)
        - unit * jnp.mean(scaled * unit, -1, keepdims=True)
    )
    return (d_values, d_gain, d_bias)


def gelu(values):
    return 0.5 * values * (1.0 + lax.erf(values * math.sqrt(0.5)))


def gelu_slope(values):
    bell = math.sqrt(0.5 / math.pi) * jnp.exp(-0.5 * values * values)
    return 0.5 * (1.0 + lax.erf(values * math.sqrt(0.5))) + values * bell


def dot(formula, left, right):
    return jnp.einsum(formula, left, right, preferred_element_type=FL)


MESH = pl.DeviceIdType.MESH
LINE = 4
GRID_DP = 16
ROWS = 368
HALVES = ((0, 192), (192, 176))


def place():
    k = lax.axis_index("dp")
    c = lax.axis_index("mp")
    z = k // 4
    y = (k // 2) % 2
    x = k % 2
    return (k, c, z, y, x, k + 2 - 4 * y, k + 1 - 2 * x)


def greet(k, c, z, y_peer, x_peer):
    barrier = pltpu.get_barrier_semaphore()

    def signal(dp, mp):
        pl.semaphore_signal(barrier, inc=1, device_id=(dp, mp), device_id_type=MESH)

    signal(k, 1 - c)
    signal(y_peer, c)
    signal(x_peer, c)

    @pl.when(z > 0)
    def _():
        signal(k - 4, c)

    @pl.when(z < LINE - 1)
    def _():
        signal(k + 4, c)

    peers = 3 + jnp.minimum(z, 1) + jnp.minimum(LINE - 1 - z, 1)
    pl.semaphore_wait(barrier, peers)


def gather_kernel(own_ref, pos_ref, all_ref, all_pos_ref, send_sem, recv_sem, local_sem):
    k, c, z, y, x, y_peer, x_peer = place()
    greet(k, c, z, y_peer, x_peer)
    targets = ((k - 4, c), (k + 4, c), (y_peer, c), (x_peer, c), (k, 1 - c))
    to_left, to_right, to_y, to_x, to_core = range(5)

    def block(lane, item, part):
        if part == 2:
            return all_pos_ref.at[lane, item]
        first, count = HALVES[part]
        return all_ref.at[lane, item, pl.ds(first, count)]

    def copy(item, part, way, from_own=False):
        target = block(c, item, part)
        source = target
        if from_own:
            source = pos_ref if part == 2 else own_ref.at[pl.ds(*HALVES[part])]
        return pltpu.make_async_remote_copy(
            src_ref=source,
            dst_ref=target,
            send_sem=send_sem.at[way, part, item],
            recv_sem=recv_sem.at[c, part, item],
            device_id=targets[way],
            device_id_type=MESH,
        )

    def arrived(lane, item, part):
        ref = block(lane, item, part)
        pltpu.make_async_copy(ref, ref, recv_sem.at[lane, part, item]).wait()

    sent = []

    def send(item, part, way, from_own=False, when=None):
        def start():
            copy(item, part, way, from_own).start()

        def finish():
            copy(item, part, way, from_own).wait_send()

        if when is None:
            start()
        else:
            pl.when(when)(start)
        return (finish, when)

    parts = (0, 1, 2)
    keep = pltpu.make_async_copy(own_ref, all_ref.at[c, k], local_sem.at[0])
    keep_pos = pltpu.make_async_copy(pos_ref, all_pos_ref.at[c, k], local_sem.at[1])
    for part in parts:
        sent.append(send(k, part, to_left, True, z > 0))
        sent.append(send(k, part, to_right, True, z < LINE - 1))
        sent.append(send(k, part, to_y, True))
        sent.append(send(k, part, to_x, True))
    for part in parts:
        sent.append(send(k, part, to_core, True))
    keep.start()
    keep_pos.start()

    first_hop = (to_y, to_x, to_y)
    second_hop = (to_x, to_y, to_x)
    first_peer = (y_peer, x_peer, y_peer)
    second_peer = (x_peer, y_peer, x_peer)
    both = k + 3 - 4 * y - 2 * x
    steps = [(0, 0)] + [(t, sign) for t in range(1, LINE) for sign in (-1, 1)]

    def valid(step):
        t, sign = step
        if t == 0:
            return None
        return z >= t if sign < 0 else z + t <= LINE - 1

    def guarded(step, action):
        when = valid(step)
        if when is None:
            action()
        else:
            pl.when(when)(action)

    finishes = []

    def stage_line(step):
        t, sign = step
        if t == 0:
            return
        shift = 4 * t * sign

        def action():
            for part in parts:
                arrived(c, k + shift, part)
                onward = to_right if sign < 0 else to_left
                copy_when = z < LINE - 1 if sign < 0 else z > 0
                send(k + shift, part, onward, when=copy_when)
                send(k + shift, part, first_hop[part])
                send(k + shift, part, second_hop[part])
                send(k + shift, part, to_core)

        guarded(step, action)

        def closing():
            for part in parts:
                onward = to_right if sign < 0 else to_left
                copy_when = z < LINE - 1 if sign < 0 else z > 0

                @pl.when(copy_when)
                def _():
                    copy(k + shift, part, onward).wait_send()

                for way in (to_y, to_x, to_core):
                    copy(k + shift, part, way).wait_send()

        finishes.append((step, closing))

    def stage_first(step):
        t, sign = step
        shift = 4 * t * sign

        def action():
            for part in parts:
                item = first_peer[part] + shift
                arrived(c, item, part)
                send(item, part, second_hop[part])
                send(item, part, to_core)

        guarded(step, action)

        def closing():
            for part in parts:
                item = first_peer[part] + shift
                for way in (second_hop[part], to_core):
                    copy(item, part, way).wait_send()

        finishes.append((step, closing))

    def stage_second(step):
        t, sign = step
        shift = 4 * t * sign

        def action():
            for part in parts:
                for peer in (second_peer[part], both):
                    arrived(c, peer + shift, part)
                    send(peer + shift, part, to_core)

        guarded(step, action)

        def closing():
            for part in parts:
                for peer in (second_peer[part], both):
                    copy(peer + shift, part, to_core).wait_send()

        finishes.append((step, closing))

    groups = [steps[0:1], steps[1:3], steps[3:5], steps[5:7]]
    for turn in range(len(groups) + 2):
        if turn < len(groups):
            for step in groups[turn]:
                stage_line(step)
        if 0 <= turn - 1 < len(groups):
            for step in groups[turn - 1]:
                stage_first(step)
        if 0 <= turn - 2 < len(groups):
            for step in groups[turn - 2]:
                stage_second(step)

    def from_core(item, carry):
        for part in parts:
            arrived(1 - c, item, part)
        return carry

    lax.fori_loop(0, GRID_DP, from_core, 0)
    for finish, when in sent:
        if when is None:
            finish()
        else:
            pl.when(when)(finish)
    for step, closing in finishes:
        guarded(step, closing)
    keep.wait()
    keep_pos.wait()


def gather_all(packed, positions):
    anywhere = pl.BlockSpec(memory_space=pl.ANY)
    return pl.pallas_call(
        gather_kernel,
        out_shape=(
            jax.ShapeDtypeStruct((2, GRID_DP) + packed.shape, packed.dtype),
            jax.ShapeDtypeStruct((2, GRID_DP) + positions.shape, positions.dtype),
        ),
        in_specs=[anywhere, anywhere],
        out_specs=(anywhere, anywhere),
        scratch_shapes=[
            pltpu.SemaphoreType.DMA((5, 3, GRID_DP)),
            pltpu.SemaphoreType.DMA((2, 3, GRID_DP)),
            pltpu.SemaphoreType.DMA((2,)),
        ],
        compiler_params=pltpu.CompilerParams(collective_id=0, has_side_effects=True),
        name="gather_weights",
    )(packed, positions)


def fetch_weights(mats, patch_embed, class_head, pos_table, norm_params):
    dp_size = lax.axis_size("dp")
    mp_size = lax.axis_size("mp")
    mp_index = lax.axis_index("mp")
    counts = [mat.shape[2] for mat in mats]
    width = mats[0].shape[1]
    classes = class_head.shape[1]
    tokens = pos_table.shape[1]
    head_rows, head_parts = class_head.shape[0], -(-classes // width)
    head = jnp.pad(class_head, ((0, 0), (0, head_parts * width - classes)))
    head = [head[:, part * width : (part + 1) * width] for part in range(head_parts)]
    matrix_rows = sum(counts)
    patch_rows = patch_embed.shape[0]
    total = -(-(matrix_rows + max(patch_rows, head_rows * head_parts)) // 16) * 16
    lead = [mat[0].T for mat in mats]

    def filled(parts):
        rows = sum([part.shape[0] for part in parts])
        return jnp.concatenate(parts + [jnp.zeros((total - rows, width), FL)], 0).astype(BF)

    packed = jnp.where(mp_index == 0, filled(lead + [patch_embed]), filled(lead + head))
    both = jnp.concatenate([pos_table, norm_params], 1)
    both = jnp.pad(both, ((0, 0), (0, 128 * mp_size - both.shape[1])))
    both = lax.dynamic_slice_in_dim(both, mp_index * 128, 128, 1)
    if dp_size == GRID_DP and total == ROWS:
        whole, table = gather_all(packed, both)
    else:
        whole = jnp.swapaxes(lax.all_gather(packed, ("dp", "mp")), 0, 0)
        whole = jnp.swapaxes(whole.reshape((dp_size, mp_size) + packed.shape), 0, 1)
        table = lax.all_gather(both, ("dp", "mp"))
        table = jnp.swapaxes(table.reshape((dp_size, mp_size) + both.shape), 0, 1)
    parts = []
    at = 0
    for count in counts:
        parts.append(whole[:, :, at : at + count].reshape(mp_size, dp_size * count, width))
        at += count
    patch_w = whole[0, :, at : at + patch_rows].reshape(dp_size * patch_rows, width)
    head_w = [
        whole[1, :, at + part * head_rows : at + (part + 1) * head_rows].reshape(width, width)
        for part in range(head_parts)
    ]
    head_w = jnp.concatenate(head_w, 1)[:, :classes]
    table = jnp.concatenate([table[0], table[1]], -1).reshape(width, 128 * mp_size).T
    return (parts, patch_w, head_w, table[:tokens], table[tokens : tokens + norm_params.shape[1]])


def local_step(images, counts, target_weight, fetched):
    (in_t, out_t, up_t, down_t), patch_w, head_w, pos_t, norm_t = fetched
    image_count = images.shape[0]
    layers, triple, width = in_t.shape
    heads = triple // 3 // HEAD_DIM
    embedded = dot("ipc,cd->ipd", images, patch_w)
    resid = jnp.concatenate([jnp.zeros((image_count, 1, width), FL), embedded], 1) + pos_t[None]
    tokens = resid.shape[1]
    saved = []
    for layer in range(layers):
        normed, unit_a, inv_a = layer_norm(resid, norm_t[4 * layer], norm_t[4 * layer + 1])
        rows_a = normed.astype(BF)
        joined = dot("itd,ed->ite", rows_a, in_t[layer]).astype(BF)
        joined = joined.reshape(image_count, tokens, 3, heads, HEAD_DIM)
        scores = dot("ithe,ishe->ihts", joined[:, :, 0], joined[:, :, 1]) * HEAD_DIM ** (-0.5)
        grown = jnp.exp(scores - jnp.max(scores, -1, keepdims=True))
        probs = grown / jnp.sum(grown, -1, keepdims=True)
        attended = dot("ihts,ishe->ithe", probs.astype(BF), joined[:, :, 2]).astype(BF)
        attended = attended.reshape(image_count, tokens, heads * HEAD_DIM)
        mid = resid + dot("ite,de->itd", attended, out_t[layer])
        normed, unit_b, inv_b = layer_norm(mid, norm_t[4 * layer + 2], norm_t[4 * layer + 3])
        rows_b = normed.astype(BF)
        pre = dot("itd,fd->itf", rows_b, up_t[layer])
        active = gelu(pre).astype(BF)
        resid = mid + dot("itf,fd->itd", active, down_t[layer])
        saved.append(
            (rows_a, unit_a, inv_a, joined, probs, attended, rows_b, unit_b, inv_b, pre, active)
        )
    normed, unit_f, inv_f = layer_norm(resid[:, 0], norm_t[4 * layers], norm_t[4 * layers + 1])
    features = normed.astype(BF)
    logits = dot("id,dc->ic", features, head_w)
    row_max = jnp.max(logits, -1, keepdims=True)
    log_total = row_max + jnp.log(jnp.sum(jnp.exp(logits - row_max), -1, keepdims=True))
    score = log_total[:, 0] - jnp.mean(logits, -1)
    loss = jnp.sum(counts * log_total[:, 0]) - jnp.sum(target_weight * logits)
    d_logits = (counts[:, None] * jnp.exp(logits - log_total) - target_weight).astype(BF)
    d_head = dot("id,ic->dc", features, d_logits)
    d_features = dot("ic,dc->id", d_logits, head_w)
    d_final, gain_f, bias_f = layer_norm_grad(d_features, unit_f, inv_f, norm_t[4 * layers])
    d_resid = jnp.zeros_like(resid).at[:, 0].set(d_final)
    d_mats = [None] * layers
    d_norm = [None] * (4 * layers) + [gain_f, bias_f]
    for layer in reversed(range(layers)):
        rows_a, unit_a, inv_a, joined, probs, attended, rows_b, unit_b, inv_b, pre, active = saved[
            layer
        ]
        upper = d_resid.astype(BF)
        d_down = dot("itf,itd->fd", active, upper)
        d_pre = (dot("itd,fd->itf", upper, down_t[layer]) * gelu_slope(pre)).astype(BF)
        d_up = dot("itf,itd->fd", d_pre, rows_b)
        d_rows = dot("itf,fd->itd", d_pre, up_t[layer])
        d_mid, d_norm[4 * layer + 2], d_norm[4 * layer + 3] = layer_norm_grad(
            d_rows, unit_b, inv_b, norm_t[4 * layer + 2]
        )
        d_mid = d_mid + d_resid
        upper = d_mid.astype(BF)
        d_out = dot("itd,ite->de", upper, attended)
        d_att = dot("itd,de->ite", upper, out_t[layer]).astype(BF)
        d_att = d_att.reshape(image_count, tokens, heads, HEAD_DIM)
        d_probs = dot("ithe,ishe->ihts", d_att, joined[:, :, 2])
        d_scores = (probs * (d_probs - jnp.sum(d_probs * probs, -1, keepdims=True))).astype(BF)
        d_value = dot("ihts,ithe->ishe", probs.astype(BF), d_att)
        d_query = dot("ihts,ishe->ithe", d_scores, joined[:, :, 1]) * HEAD_DIM ** (-0.5)
        d_keys = dot("ihts,ithe->ishe", d_scores, joined[:, :, 0]) * HEAD_DIM ** (-0.5)
        d_joined = jnp.stack([d_query, d_keys, d_value], 2).astype(BF)
        d_joined = d_joined.reshape(image_count, tokens, triple)
        d_in = dot("ite,itd->ed", d_joined, rows_a)
        d_rows = dot("ite,ed->itd", d_joined, in_t[layer])
        d_low, d_norm[4 * layer], d_norm[4 * layer + 1] = layer_norm_grad(
            d_rows, unit_a, inv_a, norm_t[4 * layer]
        )
        d_resid = d_mid + d_low
        d_mats[layer] = (d_in, d_out, d_up, d_down)
    d_patch = dot("ipc,ipd->cd", images, d_resid[:, 1:].astype(BF))
    d_pos = jnp.sum(d_resid, 0)
    return (loss, score, d_mats, d_patch, d_head, d_pos.T, jnp.stack(d_norm, 1))


def reduce_mats(d_mats):
    dp_size = lax.axis_size("dp")
    layers = []
    for mats in d_mats:
        chunks = [mat.reshape(dp_size, -1, mat.shape[1]) for mat in mats]
        layers.append(jnp.concatenate(chunks, 1))
    own = lax.psum_scatter(jnp.stack(layers), "mp", scatter_dimension=0, tiled=True)[0]
    return lax.psum_scatter(own, "dp", scatter_dimension=0, tiled=False)


def reduce_small(d_smalls):
    return [
        lax.psum(lax.psum_scatter(part, "dp", scatter_dimension=0, tiled=True), "mp")
        for part in d_smalls
    ]


def muon_factor(gram):
    size = jnp.sqrt(jnp.trace(gram)) + 1e-07
    square = gram / (size * size)
    unit = jnp.eye(gram.shape[0], dtype=FL)
    factor = None

    def product(left, right):
        return jnp.dot(left, right, precision=PRECISE)

    for turn in range(5):
        mixed = NS_A * unit + NS_B * square + NS_C * product(square, square)
        factor = mixed if factor is None else product(mixed, factor)
        if turn < 4:
            square = product(product(mixed, square), mixed)
    return factor / size


def body(
    pool_images,
    pick_rows,
    pick_weight,
    pick_label,
    in_proj,
    out_proj,
    up_proj,
    down_proj,
    in_moment,
    out_moment,
    up_moment,
    down_moment,
    patch_embed,
    class_head,
    pos_table,
    norm_params,
    patch_first,
    head_first,
    pos_first,
    norm_first,
    patch_second,
    head_second,
    pos_second,
    norm_second,
):
    mp_size = lax.axis_size("mp")
    mp_index = lax.axis_index("mp")
    dp_size = lax.axis_size("dp")
    mats = (in_proj, out_proj, up_proj, down_proj)
    smalls = (patch_embed, class_head, pos_table, norm_params)
    half = pool_images.shape[0] // mp_size
    images = lax.dynamic_slice_in_dim(pool_images, mp_index * half, half)
    own_rows = mp_index * half + jnp.arange(half, dtype=jnp.int32)
    chosen = (pick_rows[None] == own_rows[:, None]).astype(FL) * pick_weight.astype(FL)[None]
    counts = jnp.sum(chosen, 1)
    classes = jnp.arange(class_head.shape[1], dtype=jnp.int32)
    is_target = (pick_label[:, None] == classes[None]).astype(FL)
    target_weight = jnp.sum(chosen[:, :, None] * is_target[None], 1)

    fetched = fetch_weights(mats, *smalls)
    loss, score, d_mats, d_patch, d_head, d_pos, d_norm = local_step(
        images, counts, target_weight, fetched
    )
    own = reduce_mats(d_mats)
    small = reduce_small((d_patch, d_head, d_pos, d_norm))
    squares = jnp.sum(own * own) + sum([jnp.sum(grad * grad) for grad in small]) / mp_size
    summed = lax.psum(jnp.stack([loss, squares, jnp.sum(counts)]), ("dp", "mp"))
    weight_total = summed[2]
    grad_norm = jnp.sqrt(summed[1]) / weight_total
    scaling = THRESHOLD / jnp.maximum(grad_norm, THRESHOLD) / weight_total

    moments = (in_moment, out_moment, up_moment, down_moment)
    momenta_t = []
    at = 0
    for moment in moments:
        count = moment.shape[2]
        momenta_t.append(MOMENTUM * moment[0].T + own[at : at + count] * scaling)
        at += count
    grams = lax.psum(
        jnp.stack([jnp.einsum("nd,ne->de", mom, mom, precision=PRECISE) for mom in momenta_t]),
        "dp",
    )
    new_mats = []
    for index, weight in enumerate(mats):
        rate = MUON_RATES[index]
        scale = 0.2 * math.sqrt(max(weight.shape[1], weight.shape[2] * dp_size))
        change = jnp.einsum(
            "ed,ne->dn", muon_factor(grams[index]), momenta_t[index], precision=PRECISE
        )
        new_mats.append(weight * (1.0 - rate * DECAY) - rate * scale * change[None])
    new_moms = [mom.T[None] for mom in momenta_t]
    firsts = (patch_first, head_first, pos_first, norm_first)
    seconds = (patch_second, head_second, pos_second, norm_second)
    new_ws, new_fs, new_ss = ([], [], [])
    for index in range(4):
        grad = small[index] * scaling
        rate = ADAM_RATES[index]
        first = BETA_ONE * firsts[index] + (1.0 - BETA_ONE) * grad
        second = BETA_TWO * seconds[index] + (1.0 - BETA_TWO) * grad * grad
        step_size = (
            first / (1.0 - BETA_ONE**STEP) / (jnp.sqrt(second / (1.0 - BETA_TWO**STEP)) + ADAM_EPS)
        )
        new_ws.append(smalls[index] * (1.0 - rate * DECAY) - rate * step_size)
        new_fs.append(first)
        new_ss.append(second)
    return (
        summed[0],
        weight_total,
        grad_norm,
        score,
        *new_mats,
        *new_moms,
        *new_ws,
        *new_fs,
        *new_ss,
    )


def solution(mesh):
    mat = P("mp", None, "dp")
    row = P("dp", None)
    in_specs = (P("dp", None, None), P("dp"), P("dp"), P("dp")) + (mat,) * 8 + (row,) * 12
    out_specs = (P(), P(), P(), P(("dp", "mp"))) + (mat,) * 8 + (row,) * 12
    return jax.shard_map(body, mesh=mesh, in_specs=in_specs, out_specs=out_specs, check_vma=False)
```

time: 1970 us -> 1120 us (0.57)
  blocking collectives: 462 us -> 121 us
  local copies, waits for them, and re-layouts: 213 us -> 47.6 us
  matrix products: 341 us -> 186 us
  other arithmetic: 219 us -> 107 us
  waiting for transfers between devices: 634 us -> 573 us
  starting transfers between devices: 50 us -> 0.28 us
  Pallas kernels: 0 us -> 48.9 us
    unnamed x41 -> x7, waiting for transfers between devices: 364 us -> 0.12 us
    all_gather x23 -> x0, blocking collectives: 334 us -> none  [the longest x1 48 us: fetch_weights(): lax.all_gather(class_head, 'dp', axis=0, tiled=True)]
    reduce_scatter x11 -> x5, waiting for transfers between devices: 170 us -> 432 us  [the longest x3 254 us: reduce_small(): lax.psum_scatter(part, 'dp', scatter_dimension=0, tiled=True)]
    dot_general x156 -> x117, matrix products: 341 us -> 186 us  [the longest x68 98.3 us: product(): return jnp.dot(left, right, precision=PRECISE)]
    psum x1 -> x2, waiting for transfers between devices: 14.2 us -> 141 us  [the longest x1 127 us: body(): lax.psum(jnp.stack([jnp.einsum('nd,ne->de', mom, mom, precision=PRECISE)...]
    all_gather x9 -> x0, waiting for transfers between devices: 87 us -> none  [the longest x1 51.8 us: fetch_weights(): lax.all_gather(down_proj.astype(BF), 'dp', axis=2, tiled=True)]
    reduce_sum x51 -> x18, other arithmetic: 106 us -> 38.7 us  [the longest x4 24.6 us: layer_norm_grad(): d_gain = jnp.sum(upstream * unit, axes)]
    pallas_call x0 -> x1, Pallas kernels: none -> 48.9 us  [gather_all(): pl.pallas_call(gather_kernel, out_shape=(jax.ShapeDtypeStruct((2, GRID_DP...]
  transfers between devices with their start and end apart: 41 -> 7, of which waited for: 15 -> 7; matrix products, arithmetic and copies ran while one was open for 32% -> 5% of each run, Pallas kernels for 0% -> 0%
where the time goes in v1:
time: 1120 us; the launch traced here: 1110 us
  waiting for transfers between devices  573 us (51%)
  matrix products  186 us (17%)
  blocking collectives  121 us (11%)
  other arithmetic  107 us (10%)
  Pallas kernels  48.9 us (4%)
  local copies, waits for them, and re-layouts  47.6 us (4%)
  between operations  28.3 us (3%)
    reduce_scatter x3, waiting for transfers between devices, reduce_small(): lax.psum_scatter(part, 'dp', scatter_dimension=0, tiled=True)  254 us
    reduce_scatter x1, waiting for transfers between devices, reduce_mats(): return lax.psum_scatter(own, 'dp', scatter_dimension=0, tiled=False)  153 us
    psum x1, waiting for transfers between devices, body(): lax.psum(jnp.stack([jnp.einsum('nd,ne->de', mom, mom, precision=PRECISE)...  127 us
    dot_general x68, matrix products, product(): return jnp.dot(left, right, precision=PRECISE)  98.3 us
    dot_general x41, matrix products, dot(): return jnp.einsum(formula, left, right, preferred_element_type=FL)  80.2 us
    unnamed x1, blocking collectives  77 us
    pallas_call x1, Pallas kernels, gather_all(): pl.pallas_call(gather_kernel, out_shape=(jax.ShapeDtypeStruct((2, GRID_DP...  48.9 us
    psum x1, blocking collectives, body(): summed = lax.psum(jnp.stack([loss, squares, jnp.sum(counts)]), ('dp', 'mp'))  39.5 us
  transfers between devices with their start and end apart: 7, of which 7 were waited for; matrix products, arithmetic and copies ran while one was open for 5% of the time, Pallas kernels for 0%

profile of v1, /device:TPU:0, one launch (start us, length us, event | category | flops | bytes accessed | tf_op | source)
XLA Modules:
  0.0 1111.9 jit_solution(13670328239861047773)
XLA Ops:
  15.1 48.9 %gather_weights.1 = (bf16[2,16,368,384]{3,2,1,0:T(8,128)(2,1)}, f32[2,16,24,128]{3,2,1,0:T(8,128)}) custom-call(bf16[368,384]{1,0:T(8,128)(2,1)} %broadcast_select_fusion.own_ref, f32[24,128]{1,0:T(8,128)} %fusion.129.pos_ref), custom_call_target="tpu_custom_call" | custom-call | tf_op jit(solution)/shard_map/gather_weights/pallas_call | solution.py:283
  66.1 4.6 fusion.153
  73.3 2.5 fusion.155
  75.8 2.8 fusion.154
  82.7 2.5 convolution_convert_fusion.1
  85.2 4.0 copy.442
  91.5 4.1 fusion.158
  95.6 2.4 convolution_convert_fusion.3
  102.4 3.5 multiply_convert_fusion.3
  111.4 2.5 convolution_convert_fusion
  113.9 4.0 copy.458
  120.2 4.1 fusion.161
  124.3 2.4 convolution_convert_fusion.2
  134.2 2.8 multiply_convert_fusion.2
  142.6 3.2 fusion.7
  147.9 6.5 multiply_reduce_fusion.4
  161.3 3.7 convolution_bitcast_fusion.3
  165.0 3.5 multiply_reduce_fusion.1
  174.5 6.1 multiply_reduce_fusion.5
  182.8 3.3 fusion.13
  188.4 6.0 multiply_reduce_fusion.6
  194.4 2.9 fusion.149
  201.8 3.7 convolution_bitcast_fusion.2
  205.5 3.5 multiply_reduce_fusion
  215.0 6.0 multiply_reduce_fusion.7
  221.1 3.3 fusion.148
  226.7 2.5 fusion.142
  229.3 2.3 convert_bitcast_fusion
  239.6 3.3 convolution_bitcast_fusion
  247.2 3.4 maximum_bitcast_fusion.1
  256.1 3.3 maximum_bitcast_fusion
  259.4 11.1 pad_maximum_fusion
  272.5 79.3 %reduce-scatter.13.cloned.1.call-done = f32[48,384]{1,0:T(8,128)} async-done(((f32[768,384]{1,0:T(8,128)}), f32[48,384]{1,0:T(8,128)}) %reduce-scatter.13.cloned.1.call-update) | async-done | bytes 73744 | tf_op jit(solution)/shard_map/reduce_scatter | solution.py:437
  351.8 128.5 %reduce-scatter.15.cloned.1.call-done = f32[24,1000]{1,0:T(8,128)} async-done(((f32[384,1000]{1,0:T(8,128)}), f32[24,1000]{1,0:T(8,128)}) %reduce-scatter.15.cloned.1.call-update) | async-done | bytes 96016 | tf_op jit(solution)/shard_map/reduce_scatter | solution.py:437
  480.3 24.5 %reduce-scatter.9.cloned.1.call-done = f32[1,16,288,384]{3,2,1,0:T(8,128)} async-done(((f32[2,16,288,384]{3,2,1,0:T(8,128)}), f32[1,16,288,384]{3,2,1,0:T(8,128)}) %reduce-scatter.9.cloned.1.call-update) | async-done | bytes 7077904 | tf_op jit(solution)/shard_map/reduce_scatter | solution.py:431
  508.9 77.0 %all-reduce.4 = f32[384,10]{0,1:T(8,128)S(1)} all-reduce(f32[384,10]{0,1:T(8,128)S(1)} %stack.115), channel_id=7, replica_groups=mesh['dp'=16,'mp'=2] {'dp'}, use_global_device_ids=true, to_apply=%region_55.56.clone | all-reduce | flops 3840 | bytes 30720
  586.0 46.2 %reduce-scatter.17.cloned.1.call-done = f32[24,197]{1,0:T(8,128)} async-done(((f32[384,197]{1,0:T(8,128)}), f32[24,197]{1,0:T(8,128)}) %reduce-scatter.17.cloned.1.call-update) | async-done | bytes 18928 | tf_op jit(solution)/shard_map/reduce_scatter | solution.py:437
  632.2 4.0 all-reduce.5
  637.5 14.3 %all-reduce.12.cloned.1.call-done = (f32[48,384]{1,0:T(8,128)}, f32[24,1000]{1,0:T(8,128)}) async-done(((f32[48,384]{1,0:T(8,128)}, f32[24,1000]{1,0:T(8,128)}), (f32[48,384]{1,0:T(8,128)}, f32[24,1000]{1,0:T(8,128)})) %all-reduce.12.cloned.1.call-update) | async-done | bytes 169744 | tf_op jit(solution)/shard_map/psum | solution.py:437
  657.4 153.2 %reduce-scatter.11.cloned.1.call-done = f32[1,288,384]{2,1,0:T(8,128)} async-done(((f32[16,288,384]{2,1,0:T(8,128)}), f32[1,288,384]{2,1,0:T(8,128)}) %reduce-scatter.11.cloned.1.call-update) | async-done | bytes 442384 | tf_op jit(solution)/shard_map/reduce_scatter | solution.py:432
  813.7 39.5 %psum.46 = f32[3]{0:T(128)S(1)} all-reduce(f32[3]{0:T(128)S(1)} %pad_maximum_fusion.6), channel_id=1, replica_groups=mesh['dp'=16,'mp'=2] {'dp','mp'}, use_global_device_ids=true, to_apply=%region_59.60 | all-reduce | flops 3 | bytes 24 | tf_op jit(solution)/shard_map/psum | solution.py:506
  867.8 127.1 %all-reduce.10.cloned.1.call-done = f32[4,384,384]{2,1,0:T(8,128)} async-done(((f32[4,384,384]{2,1,0:T(8,128)}), f32[4,384,384]{2,1,0:T(8,128)}) %all-reduce.10.cloned.1.call-update) | async-done | bytes 2359312 | tf_op jit(solution)/shard_map/psum | solution.py:518
  994.9 2.4 fusion.80
  1008.0 3.1 fusion.27
  1011.1 2.3 fusion.113
  1020.1 2.8 fusion.32
  1031.4 2.8 fusion.37
  1034.2 2.3 fusion.115
  (521 shorter events, 205.2 us)
Async XLA Ops:
  7.2 72.0 %copy-start = (bf16[8,196,768]{2,0,1:T(8,128)(2,1)S(1)}, bf16[8,196,768]{2,0,1:T(8,128)(2,1)}, u32[]{:S(2)}) copy-start(bf16[8,196,768]{2,0,1:T(8,128)(2,1)} %param.26) | copy-start | bytes 7225348
  7.2 7.2 copy-start.94
  7.2 344.6 %reduce-scatter.13.cloned.1.call-start = ((), (), s32[]{:S(2)}) async-start(), calls=%async_computation.7 | async-start | bytes 1253376 | tf_op jit(solution)/shard_map/reduce_scatter | solution.py:437
  65.4 5.4 copy-start.48
  66.1 16.0 %copy-start.107 = (f32[384]{0:T(512)}, f32[384]{0:T(512)S(1)}, u32[]{:S(2)}) copy-start(f32[384]{0:T(512)S(1)} %get-tuple-element.136) | copy-start | bytes 4612
  75.8 6.9 copy-start.59
  98.9 3.4 copy-start.3
  102.3 3.5 copy-start.24
  102.4 3.5 copy-start.4
  102.4 3.5 copy-start.52
  130.6 3.6 copy-start.15
  138.7 3.7 copy-start.91
  138.8 3.7 copy-start.118
  139.0 3.5 copy-start.123
  161.3 3.7 copy-start.11
  161.3 3.7 copy-start.63
  161.3 3.7 copy-start.89
  161.3 7.3 slice-start.2
  165.0 3.6 slice-start.3
  172.7 10.1 slice-start.4
  174.5 6.1 copy-start.9
  174.5 8.2 slice-start.5
  182.7 3.4 copy-start.65
  194.4 3.7 copy-start.56
  201.8 3.7 copy-start.10
  201.8 3.7 copy-start.64
  201.8 3.7 copy-start.87
  201.8 7.3 slice-start
  205.5 3.6 slice-start.1
  215.0 6.1 copy-start.12
  221.1 3.5 copy-start.51
  226.6 253.6 %reduce-scatter.15.cloned.1.call-start = ((), (), s32[]{:S(2)}) async-start(), calls=%async_computation.8 | async-start | bytes 1671168 | tf_op jit(solution)/shard_map/reduce_scatter | solution.py:437
  229.2 275.7 %reduce-scatter.9.cloned.1.call-start = ((), (), s32[]{:S(2)}) async-start(), calls=%async_computation.5 | async-start | bytes 21233664 | tf_op jit(solution)/shard_map/reduce_scatter | solution.py:431
  229.2 4.4 copy-start.108
  235.0 3.5 copy-start.17
  239.6 3.9 copy-start.31
  247.2 3.4 copy-start.38
  270.5 361.7 %reduce-scatter.17.cloned.1.call-start = ((), (), s32[]{:S(2)}) async-start(), calls=%async_computation.10 | async-start | bytes 417792 | tf_op jit(solution)/shard_map/reduce_scatter | solution.py:437
  272.4 379.4 %all-reduce.12.cloned.1.call-start = ((), (), s32[]{:S(2)}) async-start(), calls=%async_computation.11 | async-start | bytes 344064 | tf_op jit(solution)/shard_map/psum | solution.py:437
  480.3 330.3 %reduce-scatter.11.cloned.1.call-start = ((), (), s32[]{:S(2)}) async-start(), calls=%async_computation.6 | async-start | bytes 7520256 | tf_op jit(solution)/shard_map/reduce_scatter | solution.py:432
  505.0 351.0 %copy-start.84 = (f32[1,384,96]{1,2,0:T(8,128)S(1)}, f32[1,384,96]{1,2,0:T(8,128)}, u32[]{:S(2)}) copy-start(f32[1,384,96]{1,2,0:T(8,128)} %param.36) | copy-start | bytes 442372
  505.0 351.0 %copy-start.85 = (f32[1,384,96]{1,2,0:T(8,128)S(1)}, f32[1,384,96]{1,2,0:T(8,128)}, u32[]{:S(2)}) copy-start(f32[1,384,96]{1,2,0:T(8,128)} %param.37) | copy-start | bytes 442372
  505.0 489.9 %all-reduce.10.cloned.1.call-start = ((), (), s32[]{:S(2)}) async-start(), calls=%async_computation.9 | async-start | bytes 4718592 | tf_op jit(solution)/shard_map/psum | solution.py:518
  505.6 352.7 %copy-start.100 = (f32[1,384,24]{1,2,0:T(8,128)S(1)}, f32[1,384,24]{1,2,0:T(8,128)}, u32[]{:S(2)}) copy-start(f32[1,384,24]{1,2,0:T(8,128)} %param.35) | copy-start | bytes 110596
  812.3 48.1 %copy-start.90 = (f32[1,384,72]{1,2,0:T(8,128)S(1)}, f32[1,384,72]{1,2,0:T(8,128)}, u32[]{:S(2)}) copy-start(f32[1,384,72]{1,2,0:T(8,128)} %param.34) | copy-start | bytes 331780
  857.0 3.5 copy-start.40
  857.0 4.4 copy-start.42
  1099.9 3.8 copy-start.1
  (106 other events, 202.8 us)
Sparse Core Ops, SparseCore 0:
  226.8 124.9 reduce-scatter.12
  356.6 123.6 reduce-scatter.14
  482.6 22.2 reduce-scatter.8
  509.4 122.8 reduce-scatter.16
  634.6 17.1 all-reduce.11
  657.8 152.6 reduce-scatter.10
  864.5 130.3 all-reduce.9
